TPU v7x, 128 devices: a whole 4x4x4 slice. The times are simulated.
128 devices in a mesh: crop: 2 (over x_lo), row: 64 (over z, y, x_hi, core).
Axes of the slice: x: 4 (x_hi: 2, x_lo: 2; x = x_hi * 2 + x_lo), y: 4, z: 4, core: 2. Of those that a mesh axis runs over, the one named last changes fastest.
Arguments:
- pair: bfloat16 [1024, 512, 128], P(('crop', 'row')), parts along dimension 0, may hold values from -6 to 6
- labels: int32 [1024, 512], P(('crop', 'row')), parts along dimension 0, may hold values from 0 to 63, as said below
- crop_length: int32 [2], P('crop'), parts along dimension 0, may hold values from 256 to 512
- in_gain: float32 [128], replicated, may hold values from 0.5 to 1.5
- in_bias: float32 [128], replicated, may hold values from -1.75 to 1.75
- proj_weight: bfloat16 [128, 512], replicated, may hold values from -0.5 to 0.5
- proj_bias: float32 [512], replicated, may hold values from -3 to 3
- gate_weight: bfloat16 [128, 128], replicated, may hold values from -0.5 to 0.5
- gate_bias: float32 [128], replicated, may hold values from -3 to 3
- mid_gain: float32 [128], replicated, may hold values from 0.5 to 1.5
- mid_bias: float32 [128], replicated, may hold values from -1.75 to 1.75
- out_weight: bfloat16 [128, 128], replicated, may hold values from -0.5 to 0.5
- out_shift: float32 [128], replicated, may hold values from -1.75 to 1.75
- dist_weight: bfloat16 [128, 64], replicated, may hold values from -33 to 33
- dist_bias: float32 [64], replicated, may hold values from -6 to 6
Outputs:
- pair_grad: bfloat16 [1024, 512, 128], P(('crop', 'row')), parts along dimension 0
- loss: float32 [2], P('crop'), parts along dimension 0
There are 2 independent parts, one for each index of `crop`. A program takes and returns all parts, laid end to end along the dimension named above; an argument that names none is the same for every part. Nothing has to cross between parts.
Inputs may be any that keep to these rules, and one draw needn't show every extreme that they name: labels[i, j] equals labels[j, i].
All inputs are finite; a program needn't handle non-finite values.
Results may differ from a plain program's by a relative error of at most 0.025.
Values may be sent and summed in bfloat16 or wider, within the bound.
A program may use at most 64 MiB of HBM per device.

v0:
```python
import jax
import jax.numpy as jnp
from jax import lax
from jax.sharding import PartitionSpec as P


def layer_norm(values, gain, shift, axis):
    mean = jnp.mean(values, axis=axis, keepdims=True)
    spread = jnp.mean((values - mean) ** 2, axis=axis, keepdims=True)
    return (values - mean) * lax.rsqrt(spread + 1e-05) * gain + shift


def project_planes(values, row_start, length, in_gain, in_bias, proj_weight, proj_bias):
    hidden = proj_weight.shape[1] // 4
    normed = layer_norm(values, in_gain, in_bias, -1).astype(jnp.bfloat16)
    proj = (
        jnp.einsum("rnc,ch->hrn", normed, proj_weight, preferred_element_type=jnp.float32)
        + proj_bias[:, None, None]
    )
    shape = (values.shape[0], values.shape[1])
    row_ids = row_start + lax.broadcasted_iota(jnp.int32, shape, 0)
    col_ids = lax.broadcasted_iota(jnp.int32, shape, 1)
    keep = ((row_ids < length) & (col_ids < length)).astype(jnp.float32)
    left = jax.nn.sigmoid(proj[:hidden]) * proj[hidden : 2 * hidden] * keep
    right = jax.nn.sigmoid(proj[2 * hidden : 3 * hidden]) * proj[3 * hidden :] * keep
    return (left.astype(jnp.bfloat16), right.astype(jnp.bfloat16))


def mix_back(
    planes,
    values,
    in_gain,
    in_bias,
    gate_weight,
    gate_bias,
    mid_gain,
    mid_bias,
    out_weight,
    out_shift,
):
    normed = layer_norm(
        planes.astype(jnp.float32), mid_gain[:, None, None], mid_bias[:, None, None], 0
    ).astype(jnp.bfloat16)
    update = (
        jnp.einsum("hrn,hc->rnc", normed, out_weight, preferred_element_type=jnp.float32)
        + out_shift
    )
    pair_norm = layer_norm(values, in_gain, in_bias, -1).astype(jnp.bfloat16)
    gate = jax.nn.sigmoid(
        jnp.einsum("rnc,cd->rnd", pair_norm, gate_weight, preferred_element_type=jnp.float32)
        + gate_bias
    )
    return (values + gate * update).astype(jnp.bfloat16)


def local(
    pair,
    labels,
    crop_length,
    in_gain,
    in_bias,
    proj_weight,
    proj_bias,
    gate_weight,
    gate_bias,
    mid_gain,
    mid_bias,
    out_weight,
    out_shift,
    dist_weight,
    dist_bias,
):
    rows, total, width = pair.shape
    bins = dist_weight.shape[1]
    row_start = lax.axis_index("row") * rows
    length = crop_length[0]
    values = pair.astype(jnp.float32)

    def first(source):
        return project_planes(source, row_start, length, in_gain, in_bias, proj_weight, proj_bias)

    def second(planes_in, source):
        return mix_back(
            planes_in,
            source,
            in_gain,
            in_bias,
            gate_weight,
            gate_bias,
            mid_gain,
            mid_bias,
            out_weight,
            out_shift,
        )

    (left, right), pull_first = jax.vjp(first, values)
    left_ch, right_ch = (
        lax.all_to_all(left, "row", split_axis=0, concat_axis=1, tiled=True),
        lax.all_to_all(right, "row", split_axis=0, concat_axis=1, tiled=True),
    )
    product = jnp.einsum(
        "hik,hjk->hij", left_ch, right_ch, preferred_element_type=jnp.float32
    ).astype(jnp.bfloat16)
    planes = lax.all_to_all(product, "row", split_axis=1, concat_axis=0, tiled=True)
    updated, pull_second = jax.vjp(second, planes, values)
    logits = (
        jnp.einsum("rnc,cb->rbn", updated, dist_weight, preferred_element_type=jnp.float32)
        + dist_bias[None, :, None]
    ).astype(jnp.bfloat16)
    mirrored = lax.all_to_all(updated, "row", split_axis=1, concat_axis=0, tiled=True)
    flipped = (
        jnp.einsum("jic,cb->ibj", mirrored, dist_weight, preferred_element_type=jnp.float32)
        + dist_bias[None, :, None]
    ).astype(jnp.bfloat16)
    sym = logits.astype(jnp.float32) + flipped.astype(jnp.float32)
    logp = jax.nn.log_softmax(sym, axis=1)
    onehot = (labels[:, None, :] == lax.broadcasted_iota(jnp.int32, (1, bins, 1), 1)).astype(
        jnp.float32
    )
    row_ids = row_start + lax.broadcasted_iota(jnp.int32, (rows, total), 0)
    col_ids = lax.broadcasted_iota(jnp.int32, (rows, total), 1)
    live = (row_ids < length) & (col_ids < length) & (row_ids != col_ids)
    upper = live & (col_ids > row_ids)
    terms = -jnp.sum(onehot * logp, axis=1)
    loss_sum = lax.psum(jnp.sum(jnp.where(upper, terms, 0.0)), "row")
    present = length.astype(jnp.float32)
    loss = (loss_sum / (present * (present - 1.0) / 2.0)).reshape(1)
    residue = jnp.where(live[:, None, :], jnp.exp(logp) - onehot, 0.0).astype(jnp.bfloat16)
    pair_cot = jnp.einsum(
        "rbn,cb->rnc", residue, dist_weight, preferred_element_type=jnp.float32
    ).astype(jnp.bfloat16)
    grad_planes, grad_mix = pull_second(pair_cot)
    grad_ch = lax.all_to_all(grad_planes, "row", split_axis=0, concat_axis=1, tiled=True)
    grad_left = jnp.einsum(
        "hij,hjk->hik", grad_ch, right_ch, preferred_element_type=jnp.float32
    ).astype(jnp.bfloat16)
    grad_right = jnp.einsum(
        "hij,hik->hjk", grad_ch, left_ch, preferred_element_type=jnp.float32
    ).astype(jnp.bfloat16)
    back_left, back_right = (
        lax.all_to_all(grad_left, "row", split_axis=1, concat_axis=0, tiled=True),
        lax.all_to_all(grad_right, "row", split_axis=1, concat_axis=0, tiled=True),
    )
    grad_first = pull_first((back_left, back_right))[0]
    return ((grad_first + grad_mix).astype(jnp.bfloat16), loss)


def solution(mesh):
    placed = (
        P(("crop", "row"), None, None),
        P(("crop", "row"), None),
        P("crop"),
        P(),
        P(),
        P(),
        P(),
        P(),
        P(),
        P(),
        P(),
        P(),
        P(),
        P(),
        P(),
    )
    return jax.shard_map(
        local,
        mesh=mesh,
        in_specs=placed,
        out_specs=(P(("crop", "row"), None, None), P("crop")),
        check_vma=False,
    )
```

profile of v0, /device:TPU:1, one launch (start us, length us, event | category | flops | bytes accessed | tf_op | source)
XLA Modules:
  0.0 411.3 jit_solution(13986091214726996531)
XLA Ops:
  3.1 2.3 fusion.24
  8.1 2.0 copy-done.1
  10.1 1.7 copy.63
  11.8 12.7 %all-to-all-start = ((bf16[128,8,512]{2,1,0:T(8,128)(2,1)}), bf16[128,8,512]{2,1,0:T(8,128)(2,1)}, u32[]{:S(2)}, u32[]{:S(2)}) async-start(bf16[128,8,512]{2,1,0:T(8,128)(2,1)} %copy.63), calls=%async_computation | async-start | bytes 2097152 | tf_op jit(solution)/shard_map/all_to_all | solution.py:98
  25.3 18.8 %all-to-all-done = bf16[128,8,512]{2,1,0:T(8,128)(2,1)} async-done(((bf16[128,8,512]{2,1,0:T(8,128)(2,1)}), bf16[128,8,512]{2,1,0:T(8,128)(2,1)}, u32[]{:S(2)}, u32[]{:S(2)}) %all-to-all-start) | async-done | bytes 1048608 | tf_op jit(solution)/shard_map/all_to_all | solution.py:98
  44.2 24.1 %all_to_all.99 = bf16[128,8,512]{2,1,0:T(8,128)(2,1)S(1)} all-to-all(bf16[128,8,512]{2,1,0:T(8,128)(2,1)S(1)} %copy.65), channel_id=1, replica_groups=mesh['crop'=2,'row'=64] {'row'}, dimensions={0} | all-to-all | bytes 2097152 | tf_op jit(solution)/shard_map/all_to_all | solution.py:99
  69.3 2.0 convolution_convert_fusion.3
  72.4 24.2 %all_to_all.100 = bf16[2,512,512]{2,0,1:T(2,128)(2,1)S(1)} all-to-all(bf16[2,512,512]{2,0,1:T(2,128)(2,1)S(1)} %copy.67), channel_id=1, replica_groups=mesh['crop'=2,'row'=64] {'row'}, dimensions={1} | all-to-all | bytes 2097152 | tf_op jit(solution)/shard_map/all_to_all | solution.py:104
  99.0 2.2 copy_bitcast_fusion
  101.1 2.7 reshape.162
  104.7 3.3 fusion.30
  108.7 24.1 %all_to_all.101 = bf16[8,512,128]{2,0,1:T(8,128)(2,1)S(1)} all-to-all(bf16[8,512,128]{2,0,1:T(8,128)(2,1)S(1)} %copy.70), channel_id=1, replica_groups=mesh['crop'=2,'row'=64] {'row'}, dimensions={1} | all-to-all | bytes 2097152 | tf_op jit(solution)/shard_map/all_to_all | solution.py:110
  134.3 3.1 fusion.57
  137.3 3.3 convolution_convert_fusion
  140.6 2.8 fusion.48
  145.9 24.1 %all_to_all.102 = bf16[128,8,512]{2,1,0:T(8,128)(2,1)S(1)} all-to-all(bf16[128,8,512]{2,1,0:T(8,128)(2,1)S(1)} %copy.72), channel_id=1, replica_groups=mesh['crop'=2,'row'=64] {'row'}, dimensions={0} | all-to-all | bytes 2097152 | tf_op jit(solution)/shard_map/all_to_all | solution.py:133
  171.1 2.0 convolution_convert_fusion.2
  173.1 2.1 copy.75
  175.1 4.6 %all-to-all-start.5 = ((bf16[2,512,512]{2,0,1:T(2,128)(2,1)}), bf16[2,512,512]{2,0,1:T(2,128)(2,1)S(1)}, u32[]{:S(2)}, u32[]{:S(2)}) async-start(bf16[2,512,512]{2,0,1:T(2,128)(2,1)} %copy.75), calls=%async_computation.5 | async-start | bytes 2097152 | tf_op jit(solution)/shard_map/all_to_all | solution.py:142
  179.8 1.9 convolution_convert_fusion.1
  181.7 2.1 copy.79
  183.9 15.8 %all-to-all-done.5 = bf16[2,512,512]{2,0,1:T(2,128)(2,1)S(1)} async-done(((bf16[2,512,512]{2,0,1:T(2,128)(2,1)}), bf16[2,512,512]{2,0,1:T(2,128)(2,1)S(1)}, u32[]{:S(2)}, u32[]{:S(2)}) %all-to-all-start.5) | async-done | bytes 1048608 | tf_op jit(solution)/shard_map/all_to_all | solution.py:142
  199.7 5.4 %all-to-all-start.6 = ((bf16[2,512,512]{2,0,1:T(2,128)(2,1)}), bf16[2,512,512]{2,0,1:T(2,128)(2,1)}, u32[]{:S(2)}, u32[]{:S(2)}) async-start(bf16[2,512,512]{2,0,1:T(2,128)(2,1)} %copy.79), calls=%async_computation.6 | async-start | bytes 2097152 | tf_op jit(solution)/shard_map/all_to_all | solution.py:141
  205.2 1.9 select_reduce_fusion
  207.8 169.3 %psum.7 = f32[]{:T(128)} all-reduce(f32[]{:T(128)} %select_reduce_fusion.1), channel_id=1, replica_groups=mesh['crop'=2,'row'=64] {'row'}, use_global_device_ids=true, to_apply=%region_17.18 | all-reduce | flops 1 | bytes 8 | tf_op jit(solution)/shard_map/psum | solution.py:125
  377.8 3.8 fusion.50
  383.3 3.0 copy.78
  389.5 2.9 copy.82
  392.4 5.7 %multiply_multiply_fusion.1 = (f32[128,8,512]{0,2,1:T(8,128)S(1)}, f32[128,8,512]{0,2,1:T(8,128)S(1)}, f32[128,8,512]{0,2,1:T(8,128)S(1)}, f32[128,8,512]{0,2,1:T(8,128)S(1)}) fusion(f32[128,8,512]{0,2,1:T(8,128)} %copy.78, f32[8,512]{1,0:T(8,128)S(1)} %get-tuple-element.20, f32[512,8,512]{0,2,1:T(8,128)} %copy-done.1, f32[128,8,512]{0,2,1:T(8,128)} %copy.82), kind=kLoop, calls=%fused_computation.76 | loop fusion | flops 9437184 | bytes 20987904 | tf_op jit(solution)/shard_map/transpose(jvp())/mul | solution.py:25
  398.1 3.8 fusion.28
  401.9 3.1 fusion.16
  405.1 5.1 %fusion.22 = bf16[8,512,128]{2,1,0:T(8,128)(2,1)} fusion(bf16[8,512,128]{2,1,0:T(8,128)(2,1)S(1)} %copy-done.4, bf16[8,512,128]{2,1,0:T(8,128)(2,1)S(1)} %copy-done.5, bf16[8,512,128]{2,1,0:T(8,128)(2,1)S(1)} %copy-done.7, bf16[8,512,128]{2,1,0:T(8,128)(2,1)S(1)} %get-tuple-element.25, f32[8,512]{1,0:T(8,128)S(1)} %get-tuple-element.26, ...), kind=kLoop, calls=%fused_computation.32 | loop fusion | flops 9437184 | bytes 5341696 | tf_op jit(solution)/shard_map/convert_element_type | solution.py:145
  (79 shorter events, 21.6 us)
Async XLA Ops:
  0.6 4.9 %copy-start = (bf16[128,512]{1,0:T(8,128)(2,1)S(1)}, bf16[128,512]{1,0:T(8,128)(2,1)}, u32[]{:S(2)}) copy-start(bf16[128,512]{1,0:T(8,128)(2,1)} %param.20) | copy-start | bytes 393220
  0.6 4.9 %copy-start.4 = (bf16[8,512,128]{2,1,0:T(8,128)(2,1)S(1)}, bf16[8,512,128]{2,1,0:T(8,128)(2,1)}, u32[]{:S(2)}) copy-start(bf16[8,512,128]{2,1,0:T(8,128)(2,1)} %param.15) | copy-start | bytes 3145732
  0.7 4.9 %copy-start.16 = (f32[128]{0:T(128)S(1)}, f32[128]{0:T(128)}, u32[]{:S(2)}) copy-start(f32[128]{0:T(128)} %param.18) | copy-start | bytes 1540
  0.7 4.9 %copy-start.20 = (f32[128]{0:T(128)S(1)}, f32[128]{0:T(128)}, u32[]{:S(2)}) copy-start(f32[128]{0:T(128)} %param.19) | copy-start | bytes 1540
  0.7 4.9 %copy-start.18 = (f32[512]{0:T(512)S(1)}, f32[512]{0:T(512)}, u32[]{:S(2)}) copy-start(f32[512]{0:T(512)} %param.21) | copy-start | bytes 6148
  6.9 3.2 copy-start.1
  11.8 32.4 %all-to-all-start = ((bf16[128,8,512]{2,1,0:T(8,128)(2,1)}), bf16[128,8,512]{2,1,0:T(8,128)(2,1)}, u32[]{:S(2)}, u32[]{:S(2)}) async-start(bf16[128,8,512]{2,1,0:T(8,128)(2,1)} %copy.63), calls=%async_computation | async-start | bytes 2097152 | tf_op jit(solution)/shard_map/all_to_all | solution.py:98
  68.3 1.0 copy-start.9
  97.4 1.5 copy-start.2
  101.1 2.7 copy-start.12
  101.1 2.8 copy-start.15
  101.1 2.8 copy-start.19
  103.9 0.8 copy-start.14
  103.9 0.8 copy-start.21
  103.9 0.7 copy-start.23
  104.7 3.3 copy-start.6
  108.0 24.8 %copy-start.8 = (bf16[8,512,128]{2,1,0:T(8,128)(2,1)}, bf16[8,512,128]{2,1,0:T(8,128)(2,1)S(1)}, u32[]{:S(2)}) copy-start(bf16[8,512,128]{2,1,0:T(8,128)(2,1)S(1)} %get-tuple-element.22) | copy-start | bytes 3145732
  108.0 24.9 %copy-start.13 = (bf16[128,64]{0,1:T(8,128)(2,1)S(1)}, bf16[128,64]{0,1:T(8,128)(2,1)}, u32[]{:S(2)}) copy-start(bf16[128,64]{0,1:T(8,128)(2,1)} %param.28) | copy-start | bytes 49156
  108.0 24.9 %copy-start.17 = (f32[64]{0:T(128)S(1)}, f32[64]{0:T(128)}, u32[]{:S(2)}) copy-start(f32[64]{0:T(128)} %param.29) | copy-start | bytes 772
  134.3 3.1 copy-start.22
  140.6 2.9 copy-start.3
  170.0 1.1 copy-start.11
  173.1 6.7 %copy-start.10 = (bf16[128,8,512]{2,1,0:T(8,128)(2,1)S(1)}, bf16[128,8,512]{2,1,0:T(8,128)(2,1)}, u32[]{:S(2)}) copy-start(bf16[128,8,512]{2,1,0:T(8,128)(2,1)} %copy-done.9) | copy-start | bytes 3145732
  175.1 24.6 %all-to-all-start.5 = ((bf16[2,512,512]{2,0,1:T(2,128)(2,1)}), bf16[2,512,512]{2,0,1:T(2,128)(2,1)S(1)}, u32[]{:S(2)}, u32[]{:S(2)}) async-start(bf16[2,512,512]{2,0,1:T(2,128)(2,1)} %copy.75), calls=%async_computation.5 | async-start | bytes 2097152 | tf_op jit(solution)/shard_map/all_to_all | solution.py:142
  183.9 193.9 %copy-start.5 = (bf16[8,512,128]{2,1,0:T(8,128)(2,1)S(1)}, bf16[8,512,128]{2,1,0:T(8,128)(2,1)}, u32[]{:S(2)}) copy-start(bf16[8,512,128]{2,1,0:T(8,128)(2,1)} %convolution_convert_fusion) | copy-start | bytes 3145732
  199.7 186.6 %all-to-all-start.6 = ((bf16[2,512,512]{2,0,1:T(2,128)(2,1)}), bf16[2,512,512]{2,0,1:T(2,128)(2,1)}, u32[]{:S(2)}, u32[]{:S(2)}) async-start(bf16[2,512,512]{2,0,1:T(2,128)(2,1)} %copy.79), calls=%async_computation.6 | async-start | bytes 2097152 | tf_op jit(solution)/shard_map/all_to_all | solution.py:141
  392.4 5.7 %copy-start.7 = (bf16[8,512,128]{2,1,0:T(8,128)(2,1)S(1)}, bf16[8,512,128]{2,1,0:T(8,128)(2,1)}, u32[]{:S(2)}) copy-start(bf16[8,512,128]{2,1,0:T(8,128)(2,1)} %fusion.50) | copy-start | bytes 3145732
where the time goes:
time: 413 us; the launch traced here: 411 us
  blocking collectives  266 us (64%)
  waiting for transfers between devices  34.7 us (8%)
  other arithmetic  29.9 us (7%)
  matrix products  29.3 us (7%)
  local copies, waits for them, and re-layouts  25.1 us (6%)
  starting transfers between devices  22.7 us (5%)
    psum x1, blocking collectives, local(): loss_sum = lax.psum(jnp.sum(jnp.where(upper, terms, 0.0)), 'row')  169 us
    all_to_all x1, blocking collectives, local(): lax.all_to_all(product, 'row', split_axis=1, concat_axis=0, tiled=True)  24.2 us
    all_to_all x1, blocking collectives, local(): lax.all_to_all(updated, 'row', split_axis=1, concat_axis=0, tiled=True)  24.1 us
    all_to_all x1, blocking collectives, local(): lax.all_to_all(grad_planes, 'row', split_axis=0, concat_axis=1, tiled=True)  24.1 us
    all_to_all x1, blocking collectives, local(): lax.all_to_all(right, 'row', split_axis=0, concat_axis=1, tiled=True)  24.1 us
    all_to_all x1, waiting for transfers between devices, local(): lax.all_to_all(left, 'row', split_axis=0, concat_axis=1, tiled=True)  18.8 us
    all_to_all x1, waiting for transfers between devices, local(): lax.all_to_all(grad_right, 'row', split_axis=1, concat_axis=0, tiled=True)  15.8 us
    all_to_all x1, starting transfers between devices, local(): lax.all_to_all(left, 'row', split_axis=0, concat_axis=1, tiled=True)  12.7 us
  transfers between devices with their start and end apart: 3, of which 2 were waited for; matrix products, arithmetic and copies ran while one was open for 4% of the time, Pallas kernels for 0%

commit v1 on v0

v1 whole, which is shorter than its diff:
```python
import jax
import jax.numpy as jnp
from jax import lax
from jax.experimental import pallas as pl
from jax.experimental.pallas import tpu as pltpu
from jax.sharding import PartitionSpec as P

MESH = pl.DeviceIdType.MESH
F32 = jnp.float32
BF16 = jnp.bfloat16
DEV = 64
ROWS = 8
N = 512
HALF = 256
CH = 128
BINS = 64


def dot(a, b):
    return jnp.dot(a, b, preferred_element_type=F32)


def spaced_store(ref, at, x):
    for t in range(x.shape[1] // 128):
        ref.at[t][pl.ds(at, CH, 16), :] = x[:, t * 128 : (t + 1) * 128]


def spaced_load(ref, at, runs):
    return jnp.concatenate([ref.at[t][pl.ds(at, CH, 16), :] for t in range(runs)], axis=1)


def tile_load(ref, at, runs):
    rows = pl.ds(pl.multiple_of(at, 16), 16)
    return jnp.concatenate([ref[t, rows, :] for t in range(runs)], axis=1)


def tile_store(ref, at, x):
    rows = pl.ds(pl.multiple_of(at, 16), 16)
    for t in range(x.shape[1] // 128):
        ref[t, rows, :] = x[:, t * 128 : (t + 1) * 128]


def partner(me, step):
    depth = lax.rem(lax.div(me, 16) + step, 4)
    height = lax.rem(lax.div(me, 4) + lax.div(step, 4) + step, 4)
    rest = lax.rem(me + lax.div(step, 16) + lax.div(step, 4) + step, 4)
    return depth * 16 + height * 4 + rest


def kernel(
    length_ref,
    pair_ref,
    labels_ref,
    in_gain_ref,
    in_bias_ref,
    proj_weight_ref,
    proj_bias_ref,
    gate_weight_ref,
    gate_bias_ref,
    mid_gain_ref,
    mid_bias_ref,
    out_weight_ref,
    out_shift_ref,
    dist_weight_ref,
    dist_bias_ref,
    grad_ref,
    loss_ref,
    values,
    in_hat,
    in_scale,
    normed,
    opened,
    amount,
    wide,
    send_planes,
    recv_planes,
    left_ch,
    right_ch,
    send_product,
    recv_product,
    mid,
    mid_hat,
    mid_scale,
    update,
    gate,
    logits,
    send_logits,
    recv_logits,
    flat_logits,
    order,
    cot,
    send_grad,
    recv_grad,
    grad_ch,
    send_back,
    recv_back,
    stack,
    part,
    parts,
    proj_t,
    gate_t,
    out_t,
    dist_t,
    back_weight,
    columns,
    proj_column,
    dist_column,
    send_sem,
    recv_sem,
):
    me = lax.axis_index("row")
    length = length_ref[0]
    first_row = me * ROWS

    def greet(step, carry):
        pl.semaphore_signal(
            pltpu.get_barrier_semaphore(),
            inc=1,
            device_id={"row": partner(me, step)},
            device_id_type=MESH,
        )
        return carry

    lax.fori_loop(1, DEV, greet, 0)

    def send(slot, source, target):
        def one(step, carry):
            peer = partner(me, step)
            pltpu.make_async_remote_copy(
                src_ref=source(peer),
                dst_ref=target,
                send_sem=send_sem.at[slot],
                recv_sem=recv_sem.at[slot],
                device_id={"row": peer},
                device_id_type=MESH,
            ).start()
            return carry

        lax.fori_loop(1, DEV, one, 0)

    def drain(slot, blocks, received):
        pltpu.make_async_copy(
            blocks, blocks, recv_sem.at[slot] if received else send_sem.at[slot]
        ).wait()

    def column(ref, out, at, size):
        out[pl.ds(at, size), :] = jnp.broadcast_to(ref[...], (8, size)).T[:, 0:1]

    column(in_gain_ref, columns, 0, CH)
    column(in_bias_ref, columns, CH, CH)
    column(gate_bias_ref, columns, 2 * CH, CH)
    column(mid_gain_ref, columns, 3 * CH, CH)
    column(mid_bias_ref, columns, 4 * CH, CH)
    column(out_shift_ref, columns, 5 * CH, CH)
    column(proj_bias_ref, proj_column, 0, 4 * CH)
    column(dist_bias_ref, dist_column, 0, BINS)
    proj_t[...] = proj_weight_ref[...].astype(F32).T.astype(BF16)
    gate_t[...] = gate_weight_ref[...].astype(F32).T.astype(BF16)
    out_t[...] = out_weight_ref[...].astype(F32).T.astype(BF16)
    dist_t[...] = dist_weight_ref[...].astype(F32).T.astype(BF16)
    back_weight[:, 0 : 4 * CH] = proj_weight_ref[...]
    back_weight[:, 4 * CH : 5 * CH] = gate_weight_ref[...]

    lane = lax.broadcasted_iota(jnp.int32, (1, N), 1)

    def kept(i):
        return jnp.where((lane < length) & (jnp.full((1, N), first_row + i) < length), 1.0, 0.0)

    def vec(k):
        return columns[pl.ds(k * CH, CH), :]

    def project(i, carry):
        x = pair_ref[i].astype(F32).T
        values[i] = x
        mean = jnp.mean(x, axis=0, keepdims=True)
        x = x - mean
        scale = lax.rsqrt(jnp.mean(x * x, axis=0, keepdims=True) + 1e-05)
        x = x * scale
        in_hat[i] = x
        in_scale[i] = scale
        norm = (x * vec(0) + vec(1)).astype(BF16)
        normed[i] = norm
        keep = kept(i)
        for side in range(2):
            at = 2 * CH * side
            proj = dot(proj_t[pl.ds(at, 2 * CH), :], norm) + proj_column[pl.ds(at, 2 * CH), :]
            open_ = jax.nn.sigmoid(proj[0:CH])
            opened[side, i] = open_
            amount[side, i] = proj[CH:]
            spaced_store(wide, side * ROWS + i, open_ * proj[CH:] * keep)
        return carry

    lax.fori_loop(0, ROWS, project, 0)

    pl.semaphore_wait(pltpu.get_barrier_semaphore(), DEV - 1)

    for odd in range(2):

        def pack(d, carry):
            send_planes[odd, d] = tile_load(wide, d * 32 + odd * 16, 4).astype(BF16)
            return carry

        lax.fori_loop(0, DEV, pack, 0)
        send(odd, lambda d: send_planes.at[odd, d], recv_planes.at[odd, me])
        recv_planes[odd, me] = send_planes[odd, me]

    def open_gate(i, carry):
        gate[i] = jax.nn.sigmoid(dot(gate_t[...], normed[i]) + vec(2))
        return carry

    lax.fori_loop(0, ROWS, open_gate, 0)
    row_at = lax.broadcasted_iota(jnp.int32, (N, N), 0)
    lane_at = lax.broadcasted_iota(jnp.int32, (N, N), 1)
    place = jnp.where(row_at < HALF, 2 * row_at, 2 * row_at - (N - 1))
    order[...] = jnp.where(place == lane_at, 1.0, 0.0).astype(BF16)

    for odd in range(2):
        drain(odd, recv_planes.at[odd, pl.ds(0, DEV - 1)], True)

        def unpack(b, carry):
            block = recv_planes[odd, pl.ds(b * 8, 8)].astype(F32).reshape(8, 2, 8, N)
            at = pl.ds(pl.multiple_of(b * 64, 64), 64)
            left_ch[odd, at, :] = block[:, 0].reshape(64, N).astype(BF16)
            right_ch[odd, at, :] = block[:, 1].reshape(64, N).astype(BF16)
            return carry

        lax.fori_loop(0, 8, unpack, 0)
        for half in range(2):
            product = lax.dot_general(
                left_ch[odd],
                right_ch[odd, half * HALF : (half + 1) * HALF, :],
                (((1,), (1,)), ((), ())),
                preferred_element_type=F32,
            )
            stack[:, half * 8 : half * 8 + 8, 0:HALF] = product.reshape(DEV, 8, HALF)
        send_product[odd] = stack[:, :, 0:HALF].astype(BF16)
        send(2 + odd, lambda d: send_product.at[odd, d], recv_product.at[odd, me])
        recv_product[odd, me] = send_product[odd, me]

    for odd in range(2):
        drain(2 + odd, recv_product.at[odd, pl.ds(0, DEV - 1)], True)

        def spread(s, carry):
            tile_store(mid, s * 32 + odd * 16, recv_product[odd, s].astype(F32))
            return carry

        lax.fori_loop(0, DEV, spread, 0)

    def mix(i, carry):
        x = jnp.concatenate([spaced_load(mid, i, 2), spaced_load(mid, 8 + i, 2)], axis=1)
        x = x - jnp.mean(x, axis=0, keepdims=True)
        scale = lax.rsqrt(jnp.mean(x * x, axis=0, keepdims=True) + 1e-05)
        x = x * scale
        mid_hat[i] = x
        mid_scale[i] = scale
        change = dot(out_t[...], (x * vec(3) + vec(4)).astype(BF16)) + vec(5)
        update[i] = change
        updated = (values[i] + gate[i] * change).astype(BF16)
        logits[i] = (dot(dist_t[...], updated) + dist_column[...]).astype(BF16).astype(F32)
        return carry

    lax.fori_loop(0, ROWS, mix, 0)

    for two in range(2):
        for low in range(2):
            p = 2 * two + low
            pairs = jnp.concatenate([logits[2 * p], logits[2 * p + 1]], axis=0).T
            stack[:, low * 8 : low * 8 + 8, 0:CH] = pairs.reshape(DEV, 8, CH)
        send_logits[:, two] = stack[:, :, 0:CH].astype(BF16)
    send(4, lambda d: send_logits.at[d], recv_logits.at[me])
    recv_logits[me] = send_logits[me]
    drain(4, recv_logits.at[pl.ds(0, DEV - 1)], True)
    flat_logits[...] = recv_logits[...].astype(F32).reshape(DEV * 32, CH)

    part[...] = jnp.zeros_like(part)
    bin_at = lax.broadcasted_iota(jnp.int32, (BINS, N), 0)

    def backward(i, carry):
        turned = flat_logits[pl.ds(i, HALF, 8), :].T.astype(BF16)
        turned = jnp.concatenate([turned[0:BINS], turned[BINS:]], axis=1)
        sym = logits[i] + dot(turned, order[...])
        sym = sym - jnp.max(sym, axis=0, keepdims=True)
        powers = jnp.exp(sym)
        logp = sym - jnp.log(jnp.sum(powers, axis=0, keepdims=True))
        hot = jnp.where(labels_ref[pl.ds(i, 1), :] == bin_at, 1.0, 0.0)
        row = jnp.full((1, N), first_row + i)
        live = (lane < length) & (row < length) & (lane != row)
        terms = -jnp.sum(hot * logp, axis=0, keepdims=True)
        terms = jnp.where(live & (lane > row), terms, 0.0)
        part[...] += (
            terms[:, 0:128] + terms[:, 128:256] + terms[:, 256:384] + terms[:, 384:512]
        )
        residue = jnp.where(live, jnp.exp(logp) - hot, 0.0).astype(BF16)
        back = dot(dist_weight_ref[...], residue).astype(BF16)
        cot[i] = back
        back = dot(out_weight_ref[...], (back.astype(F32) * gate[i]).astype(BF16)) * vec(3)
        hat = mid_hat[i]
        back = mid_scale[i] * (
            back
            - jnp.mean(back, axis=0, keepdims=True)
            - hat * jnp.mean(back * hat, axis=0, keepdims=True)
        )
        spaced_store(mid, i, back[:, 0:HALF])
        spaced_store(mid, 8 + i, back[:, HALF:])
        return carry

    lax.fori_loop(0, ROWS, backward, 0)

    for odd in range(2):

        def pack_grad(d, carry):
            send_grad[odd, d] = tile_load(mid, d * 32 + odd * 16, 2).astype(BF16)
            return carry

        lax.fori_loop(0, DEV, pack_grad, 0)
        send(5 + odd, lambda d: send_grad.at[odd, d], recv_grad.at[odd, me])
        recv_grad[odd, me] = send_grad[odd, me]

    parts[me] = part[...]
    send(7, lambda d: part, parts.at[me])

    for odd in range(2):
        drain(5 + odd, recv_grad.at[odd, pl.ds(0, DEV - 1)], True)

        def unpack_grad(b, carry):
            block = recv_grad[odd, pl.ds(b * 8, 8)].astype(F32).reshape(8, 2, 8, HALF)
            at = pl.ds(pl.multiple_of(b * 64, 64), 64)
            grad_ch[at, 0:HALF] = block[:, 0].reshape(64, HALF).astype(BF16)
            grad_ch[at, HALF:N] = block[:, 1].reshape(64, HALF).astype(BF16)
            return carry

        lax.fori_loop(0, 8, unpack_grad, 0)
        stack[:, 0:8, :] = dot(grad_ch[...], right_ch[odd]).reshape(DEV, 8, N)
        stack[:, 8:16, :] = lax.dot_general(
            grad_ch[...], left_ch[odd], (((0,), (0,)), ((), ())), preferred_element_type=F32
        ).reshape(DEV, 8, N)
        send_back[odd] = stack[...].astype(BF16)
        send(8 + odd, lambda d: send_back.at[odd, d], recv_back.at[odd, me])
        recv_back[odd, me] = send_back[odd, me]

    for odd in range(2):
        drain(8 + odd, recv_back.at[odd, pl.ds(0, DEV - 1)], True)

        def spread_back(s, carry):
            tile_store(wide, s * 32 + odd * 16, recv_back[odd, s].astype(F32))
            return carry

        lax.fori_loop(0, DEV, spread_back, 0)

    def finish(i, carry):
        keep = kept(i)
        pieces = []
        for side in range(2):
            grad = spaced_load(wide, side * ROWS + i, 4) * keep
            open_ = opened[side, i]
            grad = grad * open_
            pieces.append((grad * amount[side, i] * (1.0 - open_)).astype(BF16))
            pieces.append(grad.astype(BF16))
        back = cot[i].astype(F32)
        open_ = gate[i]
        pieces.append((back * update[i] * open_ * (1.0 - open_)).astype(BF16))
        grad = dot(back_weight[...], jnp.concatenate(pieces, axis=0)) * vec(0)
        hat = in_hat[i]
        grad = in_scale[i] * (
            grad
            - jnp.mean(grad, axis=0, keepdims=True)
            - hat * jnp.mean(grad * hat, axis=0, keepdims=True)
        )
        grad_ref[i] = (grad + back).T.astype(BF16)
        return carry

    lax.fori_loop(0, ROWS, finish, 0)

    drain(7, parts.at[pl.ds(0, DEV - 1)], True)
    total = jnp.sum(jnp.sum(parts[...], axis=0), axis=1, keepdims=True)
    present = jnp.full((1, 1), length).astype(F32)
    loss_ref[...] = jnp.broadcast_to(total / (present * (present - 1.0) / 2.0), (1, 128))

    for odd in range(2):
        drain(odd, send_planes.at[odd, pl.ds(0, DEV - 1)], False)
        drain(2 + odd, send_product.at[odd, pl.ds(0, DEV - 1)], False)
        drain(5 + odd, send_grad.at[odd, pl.ds(0, DEV - 1)], False)
        drain(8 + odd, send_back.at[odd, pl.ds(0, DEV - 1)], False)
    drain(4, send_logits.at[pl.ds(0, DEV - 1)], False)
    drain(7, parts.at[pl.ds(0, DEV - 1)], False)


SCRATCH = (
    ((ROWS, CH, N), F32),
    ((ROWS, CH, N), F32),
    ((ROWS, 1, N), F32),
    ((ROWS, CH, N), BF16),
    ((2, ROWS, CH, N), F32),
    ((2, ROWS, CH, N), F32),
    ((4, CH * 16, 128), F32),
    ((2, DEV, 16, N), BF16),
    ((2, DEV, 16, N), BF16),
    ((2, N, N), BF16),
    ((2, N, N), BF16),
    ((2, DEV, 16, HALF), BF16),
    ((2, DEV, 16, HALF), BF16),
    ((2, CH * 16, 128), F32),
    ((ROWS, CH, N), F32),
    ((ROWS, 1, N), F32),
    ((ROWS, CH, N), F32),
    ((ROWS, CH, N), F32),
    ((ROWS, BINS, N), F32),
    ((DEV, 2, 16, CH), BF16),
    ((DEV, 2, 16, CH), BF16),
    ((DEV * 32, CH), F32),
    ((N, N), BF16),
    ((ROWS, CH, N), BF16),
    ((2, DEV, 16, HALF), BF16),
    ((2, DEV, 16, HALF), BF16),
    ((N, N), BF16),
    ((2, DEV, 16, N), BF16),
    ((2, DEV, 16, N), BF16),
    ((DEV, 16, N), F32),
    ((1, 128), F32),
    ((DEV, 1, 128), F32),
    ((4 * CH, CH), BF16),
    ((CH, CH), BF16),
    ((CH, CH), BF16),
    ((BINS, CH), BF16),
    ((CH, 5 * CH), BF16),
    ((6 * CH, 1), F32),
    ((4 * CH, 1), F32),
    ((BINS, 1), F32),
)


def local(pair, labels, crop_length, *parameters):
    parameters = [p.reshape(1, -1) if p.ndim == 1 else p for p in parameters]
    grad, loss = pl.pallas_call(
        kernel,
        out_shape=(
            jax.ShapeDtypeStruct(pair.shape, BF16),
            jax.ShapeDtypeStruct((1, 128), F32),
        ),
        in_specs=[pl.BlockSpec(memory_space=pltpu.SMEM)]
        + [pl.BlockSpec(memory_space=pltpu.VMEM)] * (2 + len(parameters)),
        out_specs=[pl.BlockSpec(memory_space=pltpu.VMEM)] * 2,
        scratch_shapes=[pltpu.VMEM(shape, kind) for shape, kind in SCRATCH]
        + [pltpu.SemaphoreType.DMA((10,)), pltpu.SemaphoreType.DMA((10,))],
        compiler_params=pltpu.CompilerParams(
            collective_id=0, has_side_effects=True, vmem_limit_bytes=60 * 1024 * 1024
        ),
    )(crop_length, pair, labels, *parameters)
    return grad, loss[0, 0:1]


def solution(mesh):
    return jax.shard_map(
        local,
        mesh=mesh,
        in_specs=(P(("crop", "row"), None, None), P(("crop", "row"), None), P("crop")) + (P(),) * 12,
        out_specs=(P(("crop", "row"), None, None), P("crop")),
        check_vma=False,
    )
```

time: 413 us -> 125 us (0.30)
  blocking collectives: 266 us -> 0 us
  Pallas kernels: 0 us -> 119 us
  waiting for transfers between devices: 34.7 us -> 0 us
  other arithmetic: 29.9 us -> 0 us
  matrix products: 29.3 us -> 0 us
  starting transfers between devices: 22.7 us -> 0 us
  local copies, waits for them, and re-layouts: 25.1 us -> 3.05 us
    psum x1 -> x0, blocking collectives: 169 us -> none  [local(): loss_sum = lax.psum(jnp.sum(jnp.where(upper, terms, 0.0)), 'row')]
    pallas_call x0 -> x1, Pallas kernels: none -> 119 us  [local(): pl.pallas_call(kernel, out_shape=(jax.ShapeDtypeStruct(pair.shape, BF16),...]
    all_to_all x4 -> x0, blocking collectives: 96.6 us -> none  [the longest x1 24.2 us: local(): lax.all_to_all(product, 'row', split_axis=1, concat_axis=0, tiled=True)]
    all_to_all x3 -> x0, waiting for transfers between devices: 34.7 us -> none  [the longest x1 18.8 us: local(): lax.all_to_all(left, 'row', split_axis=0, concat_axis=1, tiled=True)]
    dot_general x11 -> x0, matrix products: 26.2 us -> none  [the longest x2 7.09 us: mix_back(): jnp.einsum('rnc,cd->rnd', pair_norm, gate_weight, preferred_element_type=...]
    all_to_all x3 -> x0, starting transfers between devices: 22.7 us -> none  [the longest x1 12.7 us: local(): lax.all_to_all(left, 'row', split_axis=0, concat_axis=1, tiled=True)]
    convert_element_type x12 -> x0, local copies, waits for them, and re-layouts: 20.9 us -> none  [the longest x6 11.6 us: project_planes(): return (left.astype(jnp.bfloat16), right.astype(jnp.bfloat16))]
    reduce_sum x8 -> x0, other arithmetic: 12.2 us -> none  [the longest x4 7.66 us: layer_norm(): spread = jnp.mean((values - mean) ** 2, axis=axis, keepdims=True)]
  transfers between devices with their start and end apart: 3 -> 0, of which waited for: 2 -> 0; matrix products, arithmetic and copies ran while one was open for 4% -> 0% of each run, Pallas kernels for 0% -> 0%
where the time goes in v1:
time: 125 us
  Pallas kernels  119 us (95%)
  local copies, waits for them, and re-layouts  3.05 us (2%)
  between operations  2.48 us (2%)
    pallas_call x1, Pallas kernels, local(): pl.pallas_call(kernel, out_shape=(jax.ShapeDtypeStruct(pair.shape, BF16),...  119 us
    unnamed x6, local copies, waits for them, and re-layouts  3.05 us

profile of v1, /device:TPU:1, one launch (start us, length us, event | category | flops | bytes accessed | tf_op | source)
XLA Modules:
  0.0 124.9 jit_solution(6516752508349974934)
XLA Ops:
  0.6 0.0 copy-start
  1.3 0.0 copy-done
  1.3 0.7 copy.17.dist_weight_ref
  2.1 119.4 %shard_map.158 = (bf16[8,512,128]{2,1,0:T(8,128)(2,1)}, f32[1,128]{1,0:T(1,128)}) custom-call(s32[1]{0:T(128)S(6)} %copy.20.length_ref, bf16[8,512,128]{2,1,0:T(8,128)(2,1)} %pair_ref.1, s32[8,512]{1,0:T(8,128)} %labels_ref.1, f32[1,128]{1,0:T(1,128)} %bitcast.11, f32[1,128]{1,0:T(1,128)} %bitcast.12, bf16[128,512]{1,0:T(8,128)(2,1)} %proj_weight_ref.1, ...), custom_call_target="tpu_custom_call" | custom-call | tf_op jit(solution)/shard_map/pallas_call | solution.py:434
  121.4 0.0 copy-start.1
  121.5 2.3 %copy.21 = bf16[8,512,128]{2,1,0:T(8,128)(2,1)} copy(bf16[8,512,128]{2,1,0:T(8,128)(2,1)} %get-tuple-element.8) | data formatting | bytes 2097152
  123.7 0.0 copy-done.1
Async XLA Ops:
  0.6 0.7 copy-start
  121.4 2.3 %copy-start.1 = (f32[1,128]{1,0:T(1,128)S(1)}, f32[1,128]{1,0:T(1,128)}, u32[]{:S(2)}) copy-start(f32[1,128]{1,0:T(1,128)} %get-tuple-element.5) | copy-start | bytes 1540

commit v2 on v1

v2 whole, which is shorter than its diff:
```python
import jax
import jax.numpy as jnp
from jax import lax
from jax.experimental import pallas as pl
from jax.experimental.pallas import tpu as pltpu
from jax.sharding import PartitionSpec as P

MESH = pl.DeviceIdType.MESH
F32 = jnp.float32
BF16 = jnp.bfloat16
DEV = 64
ROWS = 8
N = 512
HALF = 256
CH = 128
BINS = 64


def dot(a, b):
    return jnp.dot(a, b, preferred_element_type=F32)


def spaced_store(ref, at, x):
    for t in range(x.shape[1] // 128):
        ref.at[t][pl.ds(at, CH, 16), :] = x[:, t * 128 : (t + 1) * 128]


def tile_load(ref, runs, at, rows):
    rows = pl.ds(pl.multiple_of(at, 16), rows)
    return jnp.concatenate([ref[t, rows, :] for t in runs], axis=1)


def tile_store(ref, runs, at, x):
    rows = pl.ds(pl.multiple_of(at, 16), x.shape[0])
    for n, t in enumerate(runs):
        ref[t, rows, :] = x[:, n * 128 : (n + 1) * 128]


def each(count, body, unroll):
    def step(i, carry):
        body(i)
        return carry

    lax.fori_loop(0, count, step, 0, unroll=unroll)


def partner(me, step):
    depth = lax.rem(lax.div(me, 16) + step, 4)
    height = lax.rem(lax.div(me, 4) + lax.div(step, 4) + step, 4)
    rest = lax.rem(me + lax.div(step, 16) + lax.div(step, 4) + step, 4)
    return depth * 16 + height * 4 + rest


def kernel(
    length_ref,
    pair_ref,
    labels_ref,
    in_gain_ref,
    in_bias_ref,
    proj_weight_ref,
    proj_bias_ref,
    gate_weight_ref,
    gate_bias_ref,
    mid_gain_ref,
    mid_bias_ref,
    out_weight_ref,
    out_shift_ref,
    dist_turned_ref,
    dist_bias_ref,
    grad_ref,
    loss_ref,
    values,
    in_hat,
    in_scale,
    normed,
    opened,
    amount,
    wide,
    send_planes,
    recv_planes,
    send_rest,
    recv_rest,
    left_ch,
    right_ch,
    send_product,
    recv_product,
    send_second,
    recv_second,
    mid,
    mid_hat,
    mid_scale,
    update,
    gate,
    logits,
    stack,
    send_logits,
    recv_logits,
    flat_logits,
    order,
    cot,
    send_grad,
    recv_grad,
    grad_ch,
    send_back,
    recv_back,
    send_last,
    recv_last,
    part,
    parts,
    proj_t,
    gate_t,
    out_t,
    dist_weight,
    back_weight,
    columns,
    proj_column,
    dist_column,
    send_sem,
    recv_sem,
):
    me = lax.axis_index("row")
    length = length_ref[0]
    first_row = me * ROWS

    def greet(step, carry):
        pl.semaphore_signal(
            pltpu.get_barrier_semaphore(),
            inc=1,
            device_id={"row": partner(me, step)},
            device_id_type=MESH,
        )
        return carry

    lax.fori_loop(1, DEV, greet, 0)

    def send(slot, source, target, pack=None):
        def one(step, carry):
            peer = partner(me, step)
            if pack is not None:
                source.at[peer][...] = pack(peer)
            pltpu.make_async_remote_copy(
                src_ref=source.at[peer] if source.shape[0] == DEV else source,
                dst_ref=target.at[me],
                send_sem=send_sem.at[slot],
                recv_sem=recv_sem.at[slot],
                device_id={"row": peer},
                device_id_type=MESH,
            ).start()
            return carry

        lax.fori_loop(1, DEV, one, 0, unroll=3)
        if pack is not None:
            target.at[me][...] = pack(me)
        elif source.shape[0] == DEV:
            target.at[me][...] = source.at[me][...]
        else:
            target.at[me][...] = source[...]

    def arrived(slot, target):
        blocks = target.at[pl.ds(0, DEV - 1)]
        pltpu.make_async_copy(blocks, blocks, recv_sem.at[slot]).wait()

    def column(ref, out, at, size):
        out[pl.ds(at, size), :] = jnp.broadcast_to(ref[...], (8, size)).T[:, 0:1]

    column(in_gain_ref, columns, 0, CH)
    column(in_bias_ref, columns, CH, CH)
    column(proj_bias_ref, proj_column, 0, 4 * CH)
    proj_t[...] = proj_weight_ref[...].astype(F32).T.astype(BF16)

    lane = lax.broadcasted_iota(jnp.int32, (1, N), 1)

    def lanes(half):
        return slice(half * HALF, (half + 1) * HALF)

    def kept(i, half):
        row = jnp.full((1, HALF), first_row + i)
        return jnp.where((lane[:, lanes(half)] < length) & (row < length), 1.0, 0.0)

    def vec(k):
        return columns[pl.ds(k * CH, CH), :]

    def project(half):
        at = lanes(half)

        def body(i):
            x = pair_ref[i, at, :].astype(F32).T
            values[i, :, at] = x
            x = x - jnp.mean(x, axis=0, keepdims=True)
            scale = lax.rsqrt(jnp.mean(x * x, axis=0, keepdims=True) + 1e-05)
            x = x * scale
            in_hat[i, :, at] = x
            in_scale[i, :, at] = scale
            norm = (x * vec(0) + vec(1)).astype(BF16)
            normed[i, :, at] = norm
            keep = kept(i, half)
            for side in range(2):
                rows = pl.ds(2 * CH * side, 2 * CH)
                proj = dot(proj_t[rows, :], norm) + proj_column[rows, :]
                open_ = jax.nn.sigmoid(proj[0:CH])
                opened[side, i, :, at] = open_
                amount[side, i, :, at] = proj[CH:]
                spaced_store(
                    wide.at[pl.ds(2 * half, 2)], side * ROWS + i, open_ * proj[CH:] * keep
                )

        each(ROWS, body, ROWS)

    project(0)
    pl.semaphore_wait(pltpu.get_barrier_semaphore(), DEV - 1)
    send(
        0,
        send_planes,
        recv_planes,
        lambda d: tile_load(wide, (0, 1), d * 32, 32).astype(BF16).reshape(2, 16, HALF),
    )
    project(1)
    for odd in range(2):
        send(
            1 + odd,
            send_rest.at[odd],
            recv_rest.at[odd],
            lambda d: tile_load(wide, (2, 3), d * 32 + odd * 16, 16).astype(BF16),
        )

    column(gate_bias_ref, columns, 2 * CH, CH)
    column(mid_gain_ref, columns, 3 * CH, CH)
    column(mid_bias_ref, columns, 4 * CH, CH)
    column(out_shift_ref, columns, 5 * CH, CH)
    column(dist_bias_ref, dist_column, 0, BINS)
    gate_t[...] = gate_weight_ref[...].astype(F32).T.astype(BF16)
    out_t[...] = out_weight_ref[...].astype(F32).T.astype(BF16)
    dist_weight[...] = dist_turned_ref[...].astype(F32).T.astype(BF16)
    back_weight[:, 0 : 4 * CH] = proj_weight_ref[...]
    back_weight[:, 4 * CH : 5 * CH] = gate_weight_ref[...]
    row_at = lax.broadcasted_iota(jnp.int32, (N, N), 0)
    lane_at = lax.broadcasted_iota(jnp.int32, (N, N), 1)
    place = jnp.where(row_at < HALF, 2 * row_at, 2 * row_at - (N - 1))
    order[...] = jnp.where(place == lane_at, 1.0, 0.0).astype(BF16)

    def open_gate(i):
        gate[i] = jax.nn.sigmoid(dot(gate_t[...], normed[i]) + vec(2))

    each(ROWS, open_gate, 2)

    def unpack(odd, half, source):
        at = lanes(half)

        def body(b):
            block = source[pl.ds(b * 8, 8)].astype(F32).reshape(8, 2, 8, HALF)
            rows = pl.ds(pl.multiple_of(b * 64, 64), 64)
            left_ch[odd, rows, at] = block[:, 0].reshape(64, HALF).astype(BF16)
            right_ch[odd, rows, at] = block[:, 1].reshape(64, HALF).astype(BF16)

        each(8, body, 4)

    arrived(0, recv_planes)
    for odd in range(2):
        unpack(odd, 0, recv_planes.at[:, odd])

    def product(odd, half):
        x = lax.dot_general(
            left_ch[odd],
            right_ch[odd, lanes(half), :],
            (((1,), (1,)), ((), ())),
            preferred_element_type=F32,
        )
        return jnp.concatenate(
            [x[:, 0:128].reshape(DEV, 8, 128), x[:, 128:].reshape(DEV, 8, 128)], axis=1
        ).astype(BF16)

    arrived(1, recv_rest.at[0])
    unpack(0, 1, recv_rest.at[0])
    for half in range(2):
        send_product[:, half] = product(0, half)
    send(3, send_product, recv_product)
    arrived(2, recv_rest.at[1])
    unpack(1, 1, recv_rest.at[1])
    for half in range(2):
        send_second[half] = product(1, half)
        send(4 + half, send_second.at[half], recv_second.at[half])

    def mix(half):
        at = lanes(half)

        def body(i):
            x = jnp.concatenate(
                [mid.at[half][pl.ds(i, CH, 16), :], mid.at[half][pl.ds(8 + i, CH, 16), :]], axis=1
            )
            x = x - jnp.mean(x, axis=0, keepdims=True)
            scale = lax.rsqrt(jnp.mean(x * x, axis=0, keepdims=True) + 1e-05)
            x = x * scale
            mid_hat[i, :, at] = x
            mid_scale[i, :, at] = scale
            change = dot(out_t[...], (x * vec(3) + vec(4)).astype(BF16)) + vec(5)
            update[i, :, at] = change
            updated = (values[i, :, at] + gate[i, :, at] * change).astype(BF16)
            found = dot(dist_turned_ref[...], updated) + dist_column[...]
            logits[i, :, at] = found.astype(BF16).astype(F32)

        each(ROWS, body, 4)

    arrived(3, recv_product)
    for half in range(2):

        def spread(s):
            tile_store(mid, (half,), s * 32, recv_product[s, half].astype(F32))

        each(DEV, spread, 8)
    for half in range(2):
        arrived(4 + half, recv_second.at[half])

        def spread_second(s):
            tile_store(mid, (half,), s * 32 + 16, recv_second[half, s].astype(F32))

        each(DEV, spread_second, 8)
        mix(half)

    for two in range(2):
        for low in range(2):
            p = 2 * two + low
            pairs = jnp.concatenate([logits[2 * p], logits[2 * p + 1]], axis=0).T
            stack[:, low * 8 : low * 8 + 8, :] = pairs.reshape(DEV, 8, CH)
        send_logits[:, two] = stack[...].astype(BF16)
    send(6, send_logits, recv_logits)
    arrived(6, recv_logits)
    flat_logits[...] = recv_logits[...].astype(F32).reshape(DEV * 32, CH)

    part[...] = jnp.zeros_like(part)
    bin_at = lax.broadcasted_iota(jnp.int32, (BINS, HALF), 0)

    def backward(i):
        turned = flat_logits[pl.ds(i, HALF, 8), :].T.astype(BF16)
        turned = jnp.concatenate([turned[0:BINS], turned[BINS:]], axis=1)
        row = jnp.full((1, HALF), first_row + i)
        for half in range(2):
            at = lanes(half)
            sym = logits[i, :, at] + dot(turned, order[:, at])
            sym = sym - jnp.max(sym, axis=0, keepdims=True)
            logp = sym - jnp.log(jnp.sum(jnp.exp(sym), axis=0, keepdims=True))
            hot = jnp.where(labels_ref[pl.ds(i, 1), at] == bin_at, 1.0, 0.0)
            here = lane[:, at]
            live = (here < length) & (row < length) & (here != row)
            terms = -jnp.sum(hot * logp, axis=0, keepdims=True)
            terms = jnp.where(live & (here > row), terms, 0.0)
            part[...] += terms[:, 0:128] + terms[:, 128:]
            residue = jnp.where(live, jnp.exp(logp) - hot, 0.0).astype(BF16)
            back = dot(dist_weight[...], residue).astype(BF16)
            cot[i, :, at] = back
            back = (back.astype(F32) * gate[i, :, at]).astype(BF16)
            back = dot(out_weight_ref[...], back) * vec(3)
            hat = mid_hat[i, :, at]
            back = mid_scale[i, :, at] * (
                back
                - jnp.mean(back, axis=0, keepdims=True)
                - hat * jnp.mean(back * hat, axis=0, keepdims=True)
            )
            spaced_store(mid, half * 8 + i, back)

    each(ROWS, backward, ROWS)

    for odd in range(2):
        send(
            7 + odd,
            send_grad.at[odd],
            recv_grad.at[odd],
            lambda d: tile_load(mid, (0, 1), d * 32 + odd * 16, 16).astype(BF16),
        )
    send(9, part, parts)

    def planes_back(odd, half):
        at = lanes(half)
        x = dot(grad_ch[...], right_ch[odd, :, at]).reshape(DEV, 8, HALF)
        y = lax.dot_general(
            grad_ch[...], left_ch[odd, :, at], (((0,), (0,)), ((), ())), preferred_element_type=F32
        ).reshape(DEV, 8, HALF)
        return jnp.concatenate([x, y], axis=1).astype(BF16)

    for odd in range(2):
        arrived(7 + odd, recv_grad.at[odd])

        def unpack_grad(b):
            block = recv_grad[odd, pl.ds(b * 8, 8)].astype(F32).reshape(8, 2, 8, HALF)
            rows = pl.ds(pl.multiple_of(b * 64, 64), 64)
            grad_ch[rows, 0:HALF] = block[:, 0].reshape(64, HALF).astype(BF16)
            grad_ch[rows, HALF:N] = block[:, 1].reshape(64, HALF).astype(BF16)

        each(8, unpack_grad, 4)
        for half in range(2):
            if odd == 0:
                send_back[:, :, lanes(half)] = planes_back(odd, half)
            else:
                send_last[half] = planes_back(odd, half)
                send(11 + half, send_last.at[half], recv_last.at[half])
        if odd == 0:
            send(10, send_back, recv_back)

    def finish(half):
        at = lanes(half)

        def body(i):
            keep = kept(i, half)
            pieces = []
            for side in range(2):
                rows = pl.ds(side * ROWS + i, CH, 16)
                grad = jnp.concatenate(
                    [wide.at[2 * half][rows, :], wide.at[2 * half + 1][rows, :]], axis=1
                )
                open_ = opened[side, i, :, at]
                grad = grad * keep * open_
                pieces.append((grad * amount[side, i, :, at] * (1.0 - open_)).astype(BF16))
                pieces.append(grad.astype(BF16))
            back = cot[i, :, at].astype(F32)
            open_ = gate[i, :, at]
            pieces.append((back * update[i, :, at] * open_ * (1.0 - open_)).astype(BF16))
            grad = dot(back_weight[...], jnp.concatenate(pieces, axis=0)) * vec(0)
            hat = in_hat[i, :, at]
            grad = in_scale[i, :, at] * (
                grad
                - jnp.mean(grad, axis=0, keepdims=True)
                - hat * jnp.mean(grad * hat, axis=0, keepdims=True)
            )
            grad_ref[i, at, :] = (grad + back).T.astype(BF16)

        each(ROWS, body, ROWS)

    arrived(10, recv_back)

    def spread_back(s):
        tile_store(wide, (0, 1, 2, 3), s * 32, recv_back[s].astype(F32))

    each(DEV, spread_back, 8)
    for half in range(2):
        arrived(11 + half, recv_last.at[half])

        def spread_last(s):
            tile_store(
                wide, (2 * half, 2 * half + 1), s * 32 + 16, recv_last[half, s].astype(F32)
            )

        each(DEV, spread_last, 8)
        finish(half)

    arrived(9, parts)
    total = jnp.sum(jnp.sum(parts[...], axis=0), axis=1, keepdims=True)
    present = jnp.full((1, 1), length).astype(F32)
    loss_ref[...] = jnp.broadcast_to(total / (present * (present - 1.0) / 2.0), (1, 128))

    for slot, blocks in (
        (0, send_planes),
        (1, send_rest.at[0]),
        (2, send_rest.at[1]),
        (3, send_product),
        (4, send_second.at[0]),
        (5, send_second.at[1]),
        (6, send_logits),
        (7, send_grad.at[0]),
        (8, send_grad.at[1]),
        (9, parts),
        (10, send_back),
        (11, send_last.at[0]),
        (12, send_last.at[1]),
    ):
        blocks = blocks.at[pl.ds(0, DEV - 1)]
        pltpu.make_async_copy(blocks, blocks, send_sem.at[slot]).wait()


SCRATCH = (
    ((ROWS, CH, N), F32),
    ((ROWS, CH, N), F32),
    ((ROWS, 1, N), F32),
    ((ROWS, CH, N), BF16),
    ((2, ROWS, CH, N), F32),
    ((2, ROWS, CH, N), F32),
    ((4, CH * 16, 128), F32),
    ((DEV, 2, 16, HALF), BF16),
    ((DEV, 2, 16, HALF), BF16),
    ((2, DEV, 16, HALF), BF16),
    ((2, DEV, 16, HALF), BF16),
    ((2, N, N), BF16),
    ((2, N, N), BF16),
    ((DEV, 2, 16, 128), BF16),
    ((DEV, 2, 16, 128), BF16),
    ((2, DEV, 16, 128), BF16),
    ((2, DEV, 16, 128), BF16),
    ((2, CH * 16, 128), F32),
    ((ROWS, CH, N), F32),
    ((ROWS, 1, N), F32),
    ((ROWS, CH, N), F32),
    ((ROWS, CH, N), F32),
    ((ROWS, BINS, N), F32),
    ((DEV, 16, CH), F32),
    ((DEV, 2, 16, CH), BF16),
    ((DEV, 2, 16, CH), BF16),
    ((DEV * 32, CH), F32),
    ((N, N), BF16),
    ((ROWS, CH, N), BF16),
    ((2, DEV, 16, HALF), BF16),
    ((2, DEV, 16, HALF), BF16),
    ((N, N), BF16),
    ((DEV, 16, N), BF16),
    ((DEV, 16, N), BF16),
    ((2, DEV, 16, HALF), BF16),
    ((2, DEV, 16, HALF), BF16),
    ((1, 128), F32),
    ((DEV, 1, 128), F32),
    ((4 * CH, CH), BF16),
    ((CH, CH), BF16),
    ((CH, CH), BF16),
    ((CH, BINS), BF16),
    ((CH, 5 * CH), BF16),
    ((6 * CH, 1), F32),
    ((4 * CH, 1), F32),
    ((BINS, 1), F32),
)


def local(pair, labels, crop_length, *parameters):
    parameters = [p.reshape(1, -1) if p.ndim == 1 else p for p in parameters]
    parameters[10] = parameters[10].T
    grad, loss = pl.pallas_call(
        kernel,
        out_shape=(
            jax.ShapeDtypeStruct(pair.shape, BF16),
            jax.ShapeDtypeStruct((1, 128), F32),
        ),
        in_specs=[pl.BlockSpec(memory_space=pltpu.SMEM)]
        + [pl.BlockSpec(memory_space=pltpu.VMEM)] * (2 + len(parameters)),
        out_specs=[pl.BlockSpec(memory_space=pltpu.VMEM)] * 2,
        scratch_shapes=[pltpu.VMEM(shape, kind) for shape, kind in SCRATCH]
        + [pltpu.SemaphoreType.DMA((13,)), pltpu.SemaphoreType.DMA((13,))],
        compiler_params=pltpu.CompilerParams(
            collective_id=0, has_side_effects=True, vmem_limit_bytes=60 * 1024 * 1024
        ),
    )(crop_length, pair, labels, *parameters)
    return grad, loss[0, 0:1]


def solution(mesh):
    return jax.shard_map(
        local,
        mesh=mesh,
        in_specs=(P(("crop", "row"), None, None), P(("crop", "row"), None), P("crop")) + (P(),) * 12,
        out_specs=(P(("crop", "row"), None, None), P("crop")),
        check_vma=False,
    )
```

time: 125 us -> 114 us (0.912)
  Pallas kernels: 119 us -> 109 us
    pallas_call x1, Pallas kernels: 119 us -> 109 us  [local(): pl.pallas_call(kernel, out_shape=(jax.ShapeDtypeStruct(pair.shape, BF16),...]
    unnamed x6 -> x3, local copies, waits for them, and re-layouts: 3.05 us -> 2.27 us
where the time goes in v2:
time: 114 us
  Pallas kernels  109 us (96%)
  between operations  2.46 us (2%)
  local copies, waits for them, and re-layouts  2.27 us (2%)
    pallas_call x1, Pallas kernels, local(): pl.pallas_call(kernel, out_shape=(jax.ShapeDtypeStruct(pair.shape, BF16),...  109 us

profile of v2, /device:TPU:1, one launch (start us, length us, event | category | flops | bytes accessed | tf_op | source)
XLA Modules:
  0.0 113.5 jit_solution(11019217263461944685)
XLA Ops:
  1.3 108.8 %shard_map.158 = (bf16[8,512,128]{2,1,0:T(8,128)(2,1)}, f32[1,128]{1,0:T(1,128)}) custom-call(s32[1]{0:T(128)S(6)} %copy.19.length_ref, bf16[8,512,128]{2,1,0:T(8,128)(2,1)} %pair_ref.1, s32[8,512]{1,0:T(8,128)} %labels_ref.1, f32[1,128]{1,0:T(1,128)} %bitcast.13, f32[1,128]{1,0:T(1,128)} %bitcast.14, bf16[128,512]{1,0:T(8,128)(2,1)} %proj_weight_ref.1, ...), custom_call_target="tpu_custom_call" | custom-call | tf_op jit(solution)/shard_map/pallas_call | solution.py:521
  110.1 0.0 copy-start
  110.1 2.3 %copy.20 = bf16[8,512,128]{2,1,0:T(8,128)(2,1)} copy(bf16[8,512,128]{2,1,0:T(8,128)(2,1)} %get-tuple-element.8) | data formatting | bytes 2097152
  112.4 0.0 copy-done
Async XLA Ops:
  110.1 2.3 %copy-start = (f32[1,128]{1,0:T(1,128)S(1)}, f32[1,128]{1,0:T(1,128)}, u32[]{:S(2)}) copy-start(f32[1,128]{1,0:T(1,128)} %get-tuple-element.5) | copy-start | bytes 1540

commit v3 on v2

--- a/solution.py
+++ b/solution.py
@@ -44,11 +44,32 @@
     lax.fori_loop(0, count, step, 0, unroll=unroll)
 
 
+def far_first():
+    offsets = [
+        (step % 4, (step // 4 + step) % 4, (step // 16 + step // 4 + step) % 4)
+        for step in range(1, DEV)
+    ]
+    hops = lambda o: (0, 1, 2, 1)[o[0]] + (0, 1, 2, 1)[o[1]] + 2 * (o[2] // 2)
+    offsets.sort(key=lambda o: -hops(o))
+    codes = [o[0] * 16 + o[1] * 4 + o[2] for o in offsets]
+    return [
+        sum(code << (6 * n) for n, code in enumerate(codes[at : at + 5]))
+        for at in range(0, len(codes), 5)
+    ]
+
+
+WORDS = far_first()
+
+
 def partner(me, step):
-    depth = lax.rem(lax.div(me, 16) + step, 4)
-    height = lax.rem(lax.div(me, 4) + lax.div(step, 4) + step, 4)
-    rest = lax.rem(me + lax.div(step, 16) + lax.div(step, 4) + step, 4)
-    return depth * 16 + height * 4 + rest
+    at = lax.div(step - 1, 5)
+    word = jnp.int32(WORDS[0])
+    for n in range(1, len(WORDS)):
+        word = jnp.where(at == n, jnp.int32(WORDS[n]), word)
+    code = (word >> (6 * lax.rem(step - 1, 5))) & 63
+    depth = ((me >> 4) + (code >> 4)) & 3
+    height = ((me >> 2) + (code >> 2)) & 3
+    return depth * 16 + height * 4 + ((me & 3) ^ (code & 3))
 
 
 def kernel(
@@ -95,11 +116,15 @@
     stack,
     send_logits,
     recv_logits,
-    flat_logits,
     order,
+    spread_order,
+    row_order,
     cot,
+    send_first,
+    recv_first,
     send_grad,
     recv_grad,
+    grad_mixed,
     grad_ch,
     send_back,
     recv_back,
@@ -237,6 +262,10 @@
     lane_at = lax.broadcasted_iota(jnp.int32, (N, N), 1)
     place = jnp.where(row_at < HALF, 2 * row_at, 2 * row_at - (N - 1))
     order[...] = jnp.where(place == lane_at, 1.0, 0.0).astype(BF16)
+    place = (row_at & 7) * DEV + (row_at >> 3)
+    spread_order[...] = jnp.where(place == lane_at, 1.0, 0.0).astype(BF16)
+    place = ((row_at >> 2) & 1) * HALF + (row_at >> 3) * 4 + (row_at & 3)
+    row_order[...] = jnp.where(place == lane_at, 1.0, 0.0).astype(BF16)
 
     def open_gate(i):
         gate[i] = jax.nn.sigmoid(dot(gate_t[...], normed[i]) + vec(2))
@@ -316,21 +345,25 @@
         each(DEV, spread_second, 8)
         mix(half)
 
-    for two in range(2):
-        for low in range(2):
-            p = 2 * two + low
-            pairs = jnp.concatenate([logits[2 * p], logits[2 * p + 1]], axis=0).T
-            stack[:, low * 8 : low * 8 + 8, :] = pairs.reshape(DEV, 8, CH)
-        send_logits[:, two] = stack[...].astype(BF16)
-    send(6, send_logits, recv_logits)
-    arrived(6, recv_logits)
-    flat_logits[...] = recv_logits[...].astype(F32).reshape(DEV * 32, CH)
+    for p in range(4):
+        pairs = jnp.concatenate([logits[2 * p], logits[2 * p + 1]], axis=0).astype(BF16)
+        pairs = dot(pairs, spread_order[...]).T
+        for i in range(ROWS):
+            stack.at[i // 4][pl.ds(p * 4 + i % 4, DEV, 16), :] = pairs[i * DEV : (i + 1) * DEV]
+    for four in range(2):
+        send(
+            6 + 7 * four,
+            send_logits.at[four],
+            recv_logits.at[four],
+            lambda d: stack[four, pl.ds(pl.multiple_of(d * 16, 16), 16), :].astype(BF16),
+        )
 
     part[...] = jnp.zeros_like(part)
     bin_at = lax.broadcasted_iota(jnp.int32, (BINS, HALF), 0)
 
-    def backward(i):
-        turned = flat_logits[pl.ds(i, HALF, 8), :].T.astype(BF16)
+    def backward(four, b):
+        i = 4 * four + b
+        turned = stack.at[four][pl.ds(b, HALF, 4), :].T.astype(BF16)
         turned = jnp.concatenate([turned[0:BINS], turned[BINS:]], axis=1)
         row = jnp.full((1, HALF), first_row + i)
         for half in range(2):
@@ -355,16 +388,27 @@
                 - jnp.mean(back, axis=0, keepdims=True)
                 - hat * jnp.mean(back * hat, axis=0, keepdims=True)
             )
-            spaced_store(mid, half * 8 + i, back)
-
-    each(ROWS, backward, ROWS)
-
+            for t in range(2):
+                rows = pl.ds(b * 4 + 2 * half + t, CH, 16)
+                mid.at[four][rows, :] = back[:, t * 128 : (t + 1) * 128]
+
+    for four in range(2):
+        arrived(6 + 7 * four, recv_logits.at[four])
+        stack[four] = recv_logits[four].astype(F32).reshape(DEV * 16, CH)
+        each(4, lambda b: backward(four, b), 4)
+        if four == 0:
+            send(
+                14,
+                send_first,
+                recv_first,
+                lambda d: tile_load(mid, (0,), d * 32, 32).astype(BF16).reshape(2, 16, 128),
+            )
     for odd in range(2):
         send(
             7 + odd,
             send_grad.at[odd],
             recv_grad.at[odd],
-            lambda d: tile_load(mid, (0, 1), d * 32 + odd * 16, 16).astype(BF16),
+            lambda d: tile_load(mid, (1,), d * 32 + odd * 16, 16).astype(BF16),
         )
     send(9, part, parts)
 
@@ -377,15 +421,18 @@
         return jnp.concatenate([x, y], axis=1).astype(BF16)
 
     for odd in range(2):
-        arrived(7 + odd, recv_grad.at[odd])
-
-        def unpack_grad(b):
-            block = recv_grad[odd, pl.ds(b * 8, 8)].astype(F32).reshape(8, 2, 8, HALF)
-            rows = pl.ds(pl.multiple_of(b * 64, 64), 64)
-            grad_ch[rows, 0:HALF] = block[:, 0].reshape(64, HALF).astype(BF16)
-            grad_ch[rows, HALF:N] = block[:, 1].reshape(64, HALF).astype(BF16)
-
-        each(8, unpack_grad, 4)
+        for four in range(2):
+            if four == 0:
+                if odd == 0:
+                    arrived(14, recv_first)
+                stack[odd] = recv_first[:, odd].astype(F32).reshape(DEV * 16, 128)
+            else:
+                arrived(7 + odd, recv_grad.at[odd])
+                stack[odd] = recv_grad[odd].astype(F32).reshape(DEV * 16, 128)
+            for t in range(4):
+                block = stack.at[odd][pl.ds(t, HALF, 4), :]
+                grad_mixed[lanes(four), t * 128 : (t + 1) * 128] = block.astype(BF16)
+        grad_ch[...] = dot(row_order[...], grad_mixed[...]).astype(BF16)
         for half in range(2):
             if odd == 0:
                 send_back[:, :, lanes(half)] = planes_back(odd, half)
@@ -453,7 +500,9 @@
         (3, send_product),
         (4, send_second.at[0]),
         (5, send_second.at[1]),
-        (6, send_logits),
+        (6, send_logits.at[0]),
+        (13, send_logits.at[1]),
+        (14, send_first),
         (7, send_grad.at[0]),
         (8, send_grad.at[1]),
         (9, parts),
@@ -489,14 +538,18 @@
     ((ROWS, CH, N), F32),
     ((ROWS, CH, N), F32),
     ((ROWS, BINS, N), F32),
-    ((DEV, 16, CH), F32),
-    ((DEV, 2, 16, CH), BF16),
-    ((DEV, 2, 16, CH), BF16),
-    ((DEV * 32, CH), F32),
+    ((2, DEV * 16, CH), F32),
+    ((2, DEV, 16, CH), BF16),
+    ((2, DEV, 16, CH), BF16),
+    ((N, N), BF16),
+    ((N, N), BF16),
     ((N, N), BF16),
     ((ROWS, CH, N), BF16),
-    ((2, DEV, 16, HALF), BF16),
-    ((2, DEV, 16, HALF), BF16),
+    ((DEV, 2, 16, 128), BF16),
+    ((DEV, 2, 16, 128), BF16),
+    ((2, DEV, 16, 128), BF16),
+    ((2, DEV, 16, 128), BF16),
+    ((N, N), BF16),
     ((N, N), BF16),
     ((DEV, 16, N), BF16),
     ((DEV, 16, N), BF16),
@@ -528,7 +581,7 @@
         + [pl.BlockSpec(memory_space=pltpu.VMEM)] * (2 + len(parameters)),
         out_specs=[pl.BlockSpec(memory_space=pltpu.VMEM)] * 2,
         scratch_shapes=[pltpu.VMEM(shape, kind) for shape, kind in SCRATCH]
-        + [pltpu.SemaphoreType.DMA((13,)), pltpu.SemaphoreType.DMA((13,))],
+        + [pltpu.SemaphoreType.DMA((15,)), pltpu.SemaphoreType.DMA((15,))],
         compiler_params=pltpu.CompilerParams(
             collective_id=0, has_side_effects=True, vmem_limit_bytes=60 * 1024 * 1024
         ),

time: 114 us -> 111 us (0.974)
  Pallas kernels: 109 us -> 106 us
    pallas_call x1, Pallas kernels: 109 us -> 106 us  [local(): pl.pallas_call(kernel, out_shape=(jax.ShapeDtypeStruct(pair.shape, BF16),...]
where the time goes in v3:
time: 111 us
  Pallas kernels  106 us (95%)
  between operations  2.46 us (2%)
  local copies, waits for them, and re-layouts  2.27 us (2%)
    pallas_call x1, Pallas kernels, local(): pl.pallas_call(kernel, out_shape=(jax.ShapeDtypeStruct(pair.shape, BF16),...  106 us
    unnamed x3, local copies, waits for them, and re-layouts  2.27 us

profile of v3, /device:TPU:1, one launch (start us, length us, event | category | flops | bytes accessed | tf_op | source)
XLA Modules:
  0.0 111.0 jit_solution(12716361510891890309)
XLA Ops:
  1.3 106.2 %shard_map.158 = (bf16[8,512,128]{2,1,0:T(8,128)(2,1)}, f32[1,128]{1,0:T(1,128)}) custom-call(s32[1]{0:T(128)S(6)} %copy.19.length_ref, bf16[8,512,128]{2,1,0:T(8,128)(2,1)} %pair_ref.1, s32[8,512]{1,0:T(8,128)} %labels_ref.1, f32[1,128]{1,0:T(1,128)} %bitcast.13, f32[1,128]{1,0:T(1,128)} %bitcast.14, bf16[128,512]{1,0:T(8,128)(2,1)} %proj_weight_ref.1, ...), custom_call_target="tpu_custom_call" | custom-call | tf_op jit(solution)/shard_map/pallas_call | solution.py:574
  107.5 0.0 copy-start
  107.5 2.3 %copy.20 = bf16[8,512,128]{2,1,0:T(8,128)(2,1)} copy(bf16[8,512,128]{2,1,0:T(8,128)(2,1)} %get-tuple-element.8) | data formatting | bytes 2097152
  109.8 0.0 copy-done
Async XLA Ops:
  107.5 2.3 %copy-start = (f32[1,128]{1,0:T(1,128)S(1)}, f32[1,128]{1,0:T(1,128)}, u32[]{:S(2)}) copy-start(f32[1,128]{1,0:T(1,128)} %get-tuple-element.5) | copy-start | bytes 1540

commit v4 on v3

--- a/solution.py
+++ b/solution.py
@@ -53,23 +53,24 @@
     offsets.sort(key=lambda o: -hops(o))
     codes = [o[0] * 16 + o[1] * 4 + o[2] for o in offsets]
     return [
-        sum(code << (6 * n) for n, code in enumerate(codes[at : at + 5]))
-        for at in range(0, len(codes), 5)
+        sum(code << (6 * n) for n, code in enumerate(codes[at : at + 3]))
+        for at in range(0, len(codes), 3)
     ]
 
 
 WORDS = far_first()
 
 
-def partner(me, step):
-    at = lax.div(step - 1, 5)
+def partners(me, at):
     word = jnp.int32(WORDS[0])
     for n in range(1, len(WORDS)):
         word = jnp.where(at == n, jnp.int32(WORDS[n]), word)
-    code = (word >> (6 * lax.rem(step - 1, 5))) & 63
-    depth = ((me >> 4) + (code >> 4)) & 3
-    height = ((me >> 2) + (code >> 2)) & 3
-    return depth * 16 + height * 4 + ((me & 3) ^ (code & 3))
+    found = []
+    for n in range(3):
+        depth = ((me >> 4) + (word >> (6 * n + 4))) & 3
+        height = ((me >> 2) + (word >> (6 * n + 2))) & 3
+        found.append(depth * 16 + height * 4 + ((me ^ (word >> (6 * n))) & 3))
+    return found
 
 
 def kernel(
@@ -151,7 +152,7 @@
         pl.semaphore_signal(
             pltpu.get_barrier_semaphore(),
             inc=1,
-            device_id={"row": partner(me, step)},
+            device_id={"row": (me + step) & (DEV - 1)},
             device_id_type=MESH,
         )
         return carry
@@ -159,21 +160,20 @@
     lax.fori_loop(1, DEV, greet, 0)
 
     def send(slot, source, target, pack=None):
-        def one(step, carry):
-            peer = partner(me, step)
-            if pack is not None:
-                source.at[peer][...] = pack(peer)
-            pltpu.make_async_remote_copy(
-                src_ref=source.at[peer] if source.shape[0] == DEV else source,
-                dst_ref=target.at[me],
-                send_sem=send_sem.at[slot],
-                recv_sem=recv_sem.at[slot],
-                device_id={"row": peer},
-                device_id_type=MESH,
-            ).start()
-            return carry
-
-        lax.fori_loop(1, DEV, one, 0, unroll=3)
+        def three(at):
+            for peer in partners(me, at):
+                if pack is not None:
+                    source.at[peer][...] = pack(peer)
+                pltpu.make_async_remote_copy(
+                    src_ref=source.at[peer] if source.shape[0] == DEV else source,
+                    dst_ref=target.at[me],
+                    send_sem=send_sem.at[slot],
+                    recv_sem=recv_sem.at[slot],
+                    device_id={"row": peer},
+                    device_id_type=MESH,
+                ).start()
+
+        each(len(WORDS), three, 1)
         if pack is not None:
             target.at[me][...] = pack(me)
         elif source.shape[0] == DEV:
@@ -410,7 +410,6 @@
             recv_grad.at[odd],
             lambda d: tile_load(mid, (1,), d * 32 + odd * 16, 16).astype(BF16),
         )
-    send(9, part, parts)
 
     def planes_back(odd, half):
         at = lanes(half)
@@ -441,6 +440,7 @@
                 send(11 + half, send_last.at[half], recv_last.at[half])
         if odd == 0:
             send(10, send_back, recv_back)
+            send(9, part, parts)
 
     def finish(half):
         at = lanes(half)

time: 111 us -> 112 us (level)
  no operation moved by 1% of the time
where the time goes in v4:
time: 112 us
  Pallas kernels  107 us (96%)
  between operations  2.46 us (2%)
  local copies, waits for them, and re-layouts  2.27 us (2%)
    pallas_call x1, Pallas kernels, local(): pl.pallas_call(kernel, out_shape=(jax.ShapeDtypeStruct(pair.shape, BF16),...  107 us
    unnamed x3, local copies, waits for them, and re-layouts  2.27 us

profile of v4, /device:TPU:1, one launch (start us, length us, event | category | flops | bytes accessed | tf_op | source)
XLA Modules:
  0.0 111.6 jit_solution(17266996328040611118)
XLA Ops:
  1.3 106.8 %shard_map.158 = (bf16[8,512,128]{2,1,0:T(8,128)(2,1)}, f32[1,128]{1,0:T(1,128)}) custom-call(s32[1]{0:T(128)S(6)} %copy.19.length_ref, bf16[8,512,128]{2,1,0:T(8,128)(2,1)} %pair_ref.1, s32[8,512]{1,0:T(8,128)} %labels_ref.1, f32[1,128]{1,0:T(1,128)} %bitcast.13, f32[1,128]{1,0:T(1,128)} %bitcast.14, bf16[128,512]{1,0:T(8,128)(2,1)} %proj_weight_ref.1, ...), custom_call_target="tpu_custom_call" | custom-call | tf_op jit(solution)/shard_map/pallas_call | solution.py:574
  108.1 0.0 copy-start
  108.1 2.3 %copy.20 = bf16[8,512,128]{2,1,0:T(8,128)(2,1)} copy(bf16[8,512,128]{2,1,0:T(8,128)(2,1)} %get-tuple-element.8) | data formatting | bytes 2097152
  110.4 0.0 copy-done
Async XLA Ops:
  108.1 2.3 %copy-start = (f32[1,128]{1,0:T(1,128)S(1)}, f32[1,128]{1,0:T(1,128)}, u32[]{:S(2)}) copy-start(f32[1,128]{1,0:T(1,128)} %get-tuple-element.5) | copy-start | bytes 1540
